TPU v7x, 128 devices: a whole 4x4x4 slice. The times are simulated.
128 devices in a mesh: dp: 8 (over y, core), inner: 16 (over x, z).
Axes of the slice: x: 4, y: 4, z: 4, core: 2. Of those that a mesh axis runs over, the one named last changes fastest.
Arguments:
- patches: bfloat16 [49152, 1280], P(('dp', 'inner')), may hold values from -5 to 5
- segments: int32 [384, 128], P(('dp', 'inner')), may hold values from 0 to 63, as said below
- owners: int32 [384], P(('dp', 'inner')), may hold values from 0 to 7, as said below
- norm_gain: float32 [1280], replicated, may hold values from 0.1 to 1.9
- qkv_weight: bfloat16 [1280, 3840], P(('dp', 'inner')), may hold values from -0.12633784 to 0.12633784
- cotangent: bfloat16 [49152, 1280], P(('dp', 'inner')), may hold values from -6 to 6
Outputs:
- attended: bfloat16 [49152, 1280], P(('dp', 'inner'))
- grad_patches: bfloat16 [49152, 1280], P(('dp', 'inner'))
- grad_qkv: float32 [1280, 3840], P(('dp', 'inner'))
- grad_gain: float32 [1280], replicated
Inputs may be any that keep to these rules, and one draw needn't show every extreme that they name: `segments`: within a tile the ids start at 0 and grow by 0 or 1 from one patch to the next, growing only at even positions of the tile; patches of one image share an id. `owners`: the 3 tiles of one device go to 3 different groups, and for every inner index each group is owner of exactly 3 tiles.
All inputs are finite; a program needn't handle non-finite values.
Results may differ from a plain program's by a relative error of at most 0.017.
Values may be sent and summed in bfloat16 or wider, within the bound.
No kernel may reach another device: no remote copies, remote signals or barrier semaphores. Data moves between devices by JAX's collectives and lax.ppermute only.
A program may use at most 192 MiB of HBM per device.

v0:
```python
import jax
import jax.numpy as jnp
from jax import lax
from jax.sharding import PartitionSpec as P

HEADS = 16
HDIM = 80


epsilon_value = 1e-06
masked_score = -1e30


def normalize(patch_rows, norm_gain):
    widened = patch_rows.astype(jnp.float32)
    row_mean = jnp.mean(widened, axis=-1, keepdims=True)
    centred = widened - row_mean
    variance = jnp.mean(centred * centred, axis=-1, keepdims=True)
    inv_std = lax.rsqrt(variance + epsilon_value)
    standard = centred * inv_std
    normed = (standard * norm_gain).astype(jnp.bfloat16)
    return (standard, inv_std, normed)


def split_heads(qkv_tiles):
    grouped = qkv_tiles.reshape(qkv_tiles.shape[0], qkv_tiles.shape[1], 3, HEADS, HDIM)
    return (grouped[:, :, 0], grouped[:, :, 1], grouped[:, :, 2])


def attend(qkv_tiles, seg_tiles):
    queries, key_rows, values = split_heads(qkv_tiles)
    score_scale = HDIM ** (-0.5)
    scores = (
        jnp.einsum("tqhd,tkhd->thqk", queries, key_rows, preferred_element_type=jnp.float32)
        * score_scale
    )
    same_image = (seg_tiles[:, :, None] == seg_tiles[:, None, :])[:, None]
    scores = jnp.where(same_image, scores, masked_score)
    row_max = jnp.max(scores, axis=-1, keepdims=True)
    exponent = jnp.exp(scores - row_max)
    weights = exponent / jnp.sum(exponent, axis=-1, keepdims=True)
    rounded_weights = weights.astype(jnp.bfloat16)
    heads_out = jnp.einsum(
        "thqk,tkhd->tqhd", rounded_weights, values, preferred_element_type=jnp.float32
    )
    tile_out = heads_out.astype(jnp.bfloat16).reshape(
        qkv_tiles.shape[0], qkv_tiles.shape[1], HEADS * HDIM
    )
    return (tile_out, weights, rounded_weights)


def attend_back(qkv_tiles, weights, rounded_weights, d_out):
    queries, key_rows, values = split_heads(qkv_tiles)
    score_scale = HDIM ** (-0.5)
    d_heads = d_out.reshape(d_out.shape[0], d_out.shape[1], HEADS, HDIM)
    d_probs = jnp.einsum("tqhd,tkhd->thqk", d_heads, values, preferred_element_type=jnp.float32)
    d_values = jnp.einsum(
        "thqk,tqhd->tkhd", rounded_weights, d_heads, preferred_element_type=jnp.float32
    )
    row_inner = jnp.sum(d_probs * weights, axis=-1, keepdims=True)
    d_scores = (weights * (d_probs - row_inner) * score_scale).astype(jnp.bfloat16)
    d_queries = jnp.einsum(
        "thqk,tkhd->tqhd", d_scores, key_rows, preferred_element_type=jnp.float32
    )
    d_keys = jnp.einsum("thqk,tqhd->tkhd", d_scores, queries, preferred_element_type=jnp.float32)
    stacked = jnp.stack([d_queries, d_keys, d_values], axis=2)
    return stacked.astype(jnp.bfloat16).reshape(d_out.shape[0] * d_out.shape[1], 3 * HEADS * HDIM)


def on_device(patches, segments, owners, norm_gain, qkv_weight, cotangent):
    groups = lax.axis_size("dp")
    tile_count = owners.shape[0]
    tile_len = segments.shape[1]
    model_width = patches.shape[1]
    standard, inv_std, normed = normalize(patches, norm_gain)
    columns = normed
    qkv_wide = jnp.dot(
        columns,
        lax.all_gather(qkv_weight, ("dp", "inner"), axis=0, tiled=True),
        preferred_element_type=jnp.float32,
    )
    qkv = qkv_wide.astype(jnp.bfloat16).reshape(tile_count, tile_len, 3 * model_width)
    tile_out, weights, rounded_weights = attend(qkv, segments)
    group_slots = lax.broadcasted_iota(jnp.int32, (tile_count, groups), 1)
    onehot = owners[:, None] == group_slots
    onehot_bf16 = onehot.astype(jnp.bfloat16)
    sending = jnp.einsum(
        "tk,trd->krd", onehot_bf16, tile_out, preferred_element_type=jnp.float32
    ).astype(jnp.bfloat16)
    sent_flags = jnp.sum(onehot.astype(jnp.int32), axis=0)
    received, arrived = (
        lax.all_to_all(sending, "dp", split_axis=0, concat_axis=0, tiled=True),
        lax.all_to_all(sent_flags, "dp", split_axis=0, concat_axis=0, tiled=True),
    )
    arrived_order = jnp.argsort(1 - arrived, stable=True)[:tile_count]
    choose_slot = (arrived_order[:, None] == group_slots).astype(jnp.bfloat16)
    attended = jnp.einsum("pk,krd->prd", choose_slot, received, preferred_element_type=jnp.float32)
    attended = attended.astype(jnp.bfloat16).reshape(tile_count * tile_len, model_width)
    cotangent_tiles = cotangent.reshape(tile_count, tile_len, model_width)
    returning = jnp.einsum(
        "pk,prd->krd", choose_slot, cotangent_tiles, preferred_element_type=jnp.float32
    ).astype(jnp.bfloat16)
    came_back = lax.all_to_all(returning, "dp", split_axis=0, concat_axis=0, tiled=True)
    d_out = jnp.einsum(
        "tk,krd->trd", onehot_bf16, came_back, preferred_element_type=jnp.float32
    ).astype(jnp.bfloat16)
    d_qkv = attend_back(qkv, weights, rounded_weights, d_out)
    d_normed = lax.dot_general(
        d_qkv,
        lax.all_gather(qkv_weight, ("dp", "inner"), axis=0, tiled=True),
        (((1,), (1,)), ((), ())),
        preferred_element_type=jnp.float32,
    )
    columns = normed
    grad_qkv = lax.psum_scatter(
        lax.dot_general(
            columns, d_qkv, (((0,), (0,)), ((), ())), preferred_element_type=jnp.float32
        ),
        ("dp", "inner"),
        scatter_dimension=0,
        tiled=True,
    )
    grad_gain = lax.psum(jnp.sum(d_normed * standard, axis=0), ("dp", "inner"))
    scaled = d_normed * norm_gain
    grad_rows = inv_std * (
        scaled
        - jnp.mean(scaled, axis=-1, keepdims=True)
        - standard * jnp.mean(scaled * standard, axis=-1, keepdims=True)
    )
    return (attended, grad_rows.astype(jnp.bfloat16), grad_qkv, grad_gain)


def solution(mesh):
    placed = (
        P(("dp", "inner"), None),
        P(("dp", "inner"), None),
        P(("dp", "inner")),
        P(),
        P(("dp", "inner"), None),
        P(("dp", "inner"), None),
    )
    return jax.shard_map(
        on_device,
        mesh=mesh,
        in_specs=placed,
        out_specs=(
            P(("dp", "inner"), None),
            P(("dp", "inner"), None),
            P(("dp", "inner"), None),
            P(),
        ),
        check_vma=False,
    )
```

profile of v0, /device:TPU:1, one launch (start us, length us, event | category | flops | bytes accessed | tf_op | source)
XLA Modules:
  0.0 435.4 jit_solution(9792032145116246925)
XLA Ops:
  8.7 10.3 %all_to_all.19 = s32[8,1,1]{2,1,0:T(1,128)S(1)} all-to-all(s32[8,1,1]{2,1,0:T(1,128)S(1)} %copy.48), channel_id=1, replica_groups=mesh['dp'=8,'inner'=16] {'dp'}, dimensions={0} | all-to-all | bytes 64 | tf_op jit(solution)/shard_map/all_to_all | solution.py:93
  23.7 5.1 %all-to-all-start.2 = ((bf16[8,128,1280]{2,1,0:T(8,128)(2,1)}), bf16[8,128,1280]{2,1,0:T(8,128)(2,1)}, u32[]{:S(2)}, u32[]{:S(2)}) async-start(bf16[8,128,1280]{2,1,0:T(8,128)(2,1)} %copy.59), calls=%async_computation.2 | async-start | bytes 5242880 | tf_op jit(solution)/shard_map/all_to_all | solution.py:103
  30.2 36.8 %all-to-all-done.2 = bf16[8,128,1280]{2,1,0:T(8,128)(2,1)} async-done(((bf16[8,128,1280]{2,1,0:T(8,128)(2,1)}), bf16[8,128,1280]{2,1,0:T(8,128)(2,1)}, u32[]{:S(2)}, u32[]{:S(2)}) %all-to-all-start.2) | async-done | bytes 2621472 | tf_op jit(solution)/shard_map/all_to_all | solution.py:103
  67.0 3.5 convolution_convert_fusion.3
  70.5 2.2 copy.61
  72.8 30.3 %all-gather.3.cloned.1.call-done = bf16[128,10,3840]{2,1,0:T(8,128)(2,1)} async-done(((bf16[1,10,3840]{2,1,0:T(8,128)(2,1)}), bf16[128,10,3840]{2,1,0:T(8,128)(2,1)}) %all-gather.3.cloned.1.call-update) | async-done | bytes 9830416 | tf_op jit(solution)/shard_map/all_gather | solution.py:79
  103.0 15.7 %reshape.61 = bf16[1280,3840]{1,0:T(8,128)(2,1)} reshape(bf16[128,10,3840]{2,1,0:T(8,128)(2,1)} %all-gather.3.cloned.1.call-done) | data formatting | bytes 19660800
  118.7 9.3 %convolution_convert_fusion = bf16[384,3840]{1,0:T(8,128)(2,1)} fusion(bf16[1280,3840]{1,0:T(8,128)(2,1)} %reshape.61, bf16[384,1280]{1,0:T(8,128)(2,1)S(1)} %copy-done.2, f32[1280]{0:T(1024)S(1)} %copy-done.6, f32[384]{0:T(512)S(1)} %add_rsqrt_fusion, f32[384]{0:T(512)S(1)} %broadcast_multiply_fusion.2), kind=kOutput, calls=%fused_computation.2 | convolution fusion | flops 3778805760 | bytes 13770752 | tf_op jit(solution)/shard_map/dot_general | solution.py:77
  128.0 10.1 %reshape.64 = bf16[3,128,3,16,80]{4,3,2,1,0:T(8,128)(2,1)} reshape(bf16[384,3840]{1,0:T(8,128)(2,1)} %convolution_convert_fusion) | data formatting | bytes 5898240 | tf_op jit(solution)/shard_map/reshape;reshape | solution.py:26
  138.1 5.0 %fusion.80 = (bf16[3,128,1,16,80]{4,3,2,1,0:T(8,128)(2,1)S(1)}, bf16[3,128,1,16,80]{4,3,2,1,0:T(8,128)(2,1)}, bf16[3,128,1,16,80]{4,3,2,1,0:T(8,128)(2,1)}) fusion(bf16[3,128,3,16,80]{4,3,2,1,0:T(8,128)(2,1)} %reshape.64), kind=kLoop, calls=%fused_computation.86 | loop fusion | bytes 5898240 | tf_op jit(solution)/shard_map/slice | solution.py:27
  145.0 2.7 copy.74
  152.9 2.5 fusion.57
  157.5 7.2 %fusion.45 = bf16[3,128,1,16,80]{1,4,3,0,2:T(8,128)(2,1)} fusion(f32[3,16,128,128]{2,3,1,0:T(8,128)} %fusion.57, bf16[3,128,1,16,80]{1,4,3,0,2:T(8,128)(2,1)} %copy.73, f32[3,16,128,128]{2,3,1,0:T(8,128)} %copy-done.13, f32[3,16,128]{2,1,0:T(8,128)S(1)} %get-tuple-element.12), kind=kOutput, calls=%fused_computation.51 | convolution fusion | flops 131831936 | bytes 8282112 | tf_op jit(solution)/shard_map/thqk,tqhd->tkhd/dot_general | solution.py:65
  164.7 6.8 %fusion.48 = bf16[3,128,1,16,80]{1,4,3,0,2:T(8,128)(2,1)} fusion(f32[3,16,128,128]{2,3,1,0:T(8,128)} %fusion.57, bf16[3,128,1,16,80]{1,4,3,0,2:T(8,128)(2,1)S(1)} %copy-done.5, f32[3,16,128,128]{2,3,1,0:T(8,128)} %copy-done.13, f32[3,16,128]{2,1,0:T(8,128)S(1)} %get-tuple-element.12), kind=kOutput, calls=%fused_computation.52 | convolution fusion | flops 131831936 | bytes 8282112 | tf_op jit(solution)/shard_map/thqk,tkhd->tqhd/dot_general | solution.py:62
  173.6 2.5 copy.65
  177.9 9.6 %fusion.3 = f32[1280,3840]{1,0:T(8,128)} fusion(bf16[480,8,3,128]{3,2,1,0:T(4,128)(2,1)S(1)} %bitcast.61, bf16[384,1280]{1,0:T(8,128)(2,1)S(1)} %copy-done.2, f32[1280]{0:T(1024)S(1)} %copy-done.6, f32[384]{0:T(512)S(1)} %add_rsqrt_fusion, f32[384]{0:T(512)S(1)} %broadcast_multiply_fusion.2), kind=kOutput, calls=%fused_computation.12 | convolution fusion | flops 3777331200 | bytes 23601152 | tf_op jit(solution)/shard_map/dot_general | solution.py:116
  187.6 3.5 convolution_convert_fusion.6
  191.1 2.9 copy.54
  197.3 4.6 %all-to-all-start.1 = ((bf16[8,128,1280]{2,1,0:T(8,128)(2,1)}), bf16[8,128,1280]{2,1,0:T(8,128)(2,1)}, u32[]{:S(2)}, u32[]{:S(2)}) async-start(bf16[8,128,1280]{2,1,0:T(8,128)(2,1)} %copy.55), calls=%async_computation.1 | async-start | bytes 5242880 | tf_op jit(solution)/shard_map/all_to_all | solution.py:92
  201.9 11.0 %fusion.31 = (f32[1280]{0:T(1024)S(1)}, f32[384]{0:T(512)S(1)}, f32[384]{0:T(512)S(1)}, f32[384,1280]{1,0:T(8,128)}) fusion(bf16[384,1280]{1,0:T(8,128)(2,1)S(1)} %copy-done.2, f32[384]{0:T(512)S(1)} %add_rsqrt_fusion, f32[384]{0:T(512)S(1)} %broadcast_multiply_fusion.2, f32[1280]{0:T(1024)S(1)} %copy-done.6, bf16[1280,3840]{1,0:T(8,128)(2,1)} %reshape.61, ...), kind=kOutput, calls=%fused_computation.37 | convolution fusion | flops 3779295232 | bytes 15745024 | tf_op jit(solution)/shard_map/dot_general | solution.py:108
  212.9 90.4 %psum.7 = f32[1280]{0:T(1024)} all-reduce(f32[1280]{0:T(1024)S(1)} %get-tuple-element.6), channel_id=1, replica_groups=mesh['dp'=8,'inner'=16] {'dp','inner'}, use_global_device_ids=true, to_apply=%region_11.12 | all-reduce | flops 1280 | bytes 10240 | tf_op jit(solution)/shard_map/psum | solution.py:123
  303.4 3.2 fusion.30
  306.6 3.6 convolution_convert_fusion.4
  311.2 115.7 %all-reduce.3.cloned.1.call-done = f32[1280,3840]{1,0:T(8,128)} async-done(((f32[1280,3840]{1,0:T(8,128)}), f32[1280,3840]{1,0:T(8,128)}) %all-reduce.3.cloned.1.call-update) | async-done | bytes 19660816
  (56 shorter events, 26.9 us)
Async XLA Ops:
  7.2 13.1 %copy-start = (bf16[384,1280]{1,0:T(8,128)(2,1)S(1)}, bf16[384,1280]{1,0:T(8,128)(2,1)}, u32[]{:S(2)}) copy-start(bf16[384,1280]{1,0:T(8,128)(2,1)} %param.11) | copy-start | bytes 2949124
  7.2 95.8 %all-gather.3.cloned.1.call-start = ((), (), s32[]{:S(2)}) async-start(), calls=%async_computation.3 | async-start | bytes 15851520 | tf_op jit(solution)/shard_map/all_gather | solution.py:79
  20.3 1.5 copy-start.11
  23.7 5.1 %copy-start.2 = (bf16[384,1280]{1,0:T(8,128)(2,1)S(1)}, bf16[384,1280]{1,0:T(8,128)(2,1)}, u32[]{:S(2)}) copy-start(bf16[384,1280]{1,0:T(8,128)(2,1)} %param.6) | copy-start | bytes 2949124
  23.7 5.7 %copy-start.8 = (s32[3,128]{1,0:T(4,128)S(1)}, s32[3,128]{1,0:T(4,128)}, u32[]{:S(2)}) copy-start(s32[3,128]{1,0:T(4,128)} %param.7) | copy-start | bytes 4612
  23.7 43.3 %copy-start.9 = (s32[3]{0:T(128)S(1)}, s32[3]{0:T(128)}, u32[]{:S(2)}) copy-start(s32[3]{0:T(128)} %param.8) | copy-start | bytes 40
  23.7 43.3 %all-to-all-start.2 = ((bf16[8,128,1280]{2,1,0:T(8,128)(2,1)}), bf16[8,128,1280]{2,1,0:T(8,128)(2,1)}, u32[]{:S(2)}, u32[]{:S(2)}) async-start(bf16[8,128,1280]{2,1,0:T(8,128)(2,1)} %copy.59), calls=%async_computation.2 | async-start | bytes 5242880 | tf_op jit(solution)/shard_map/all_to_all | solution.py:103
  28.8 398.0 %all-reduce.3.cloned.1.call-start = ((), (), s32[]{:S(2)}) async-start(), calls=%async_computation.4 | async-start | bytes 39321600
  72.7 45.9 %copy-start.6 = (f32[1280]{0:T(1024)S(1)}, f32[1280]{0:T(1024)}, u32[]{:S(2)}) copy-start(f32[1280]{0:T(1024)} %param.9) | copy-start | bytes 15364
  149.5 2.1 copy-start.7
  151.7 1.2 copy-start.4
  152.8 2.6 copy-start.13
  157.5 7.2 %copy-start.5 = (bf16[3,128,1,16,80]{1,4,3,0,2:T(8,128)(2,1)S(1)}, bf16[3,128,1,16,80]{1,4,3,0,2:T(8,128)(2,1)}, u32[]{:S(2)}) copy-start(bf16[3,128,1,16,80]{1,4,3,0,2:T(8,128)(2,1)} %copy.74) | copy-start | bytes 2949124
  176.1 1.9 copy-start.3
  187.6 6.4 %copy-start.10 = (s32[3]{0:T(128)S(1)}, s32[3]{0:T(128)}, u32[]{:S(2)}) copy-start(s32[3]{0:T(128)} %param.8) | copy-start | bytes 40
  197.3 109.3 %all-to-all-start.1 = ((bf16[8,128,1280]{2,1,0:T(8,128)(2,1)}), bf16[8,128,1280]{2,1,0:T(8,128)(2,1)}, u32[]{:S(2)}, u32[]{:S(2)}) async-start(bf16[8,128,1280]{2,1,0:T(8,128)(2,1)} %copy.55), calls=%async_computation.1 | async-start | bytes 5242880 | tf_op jit(solution)/shard_map/all_to_all | solution.py:92
  212.9 93.6 %copy-start.12 = (s32[8]{0:T(128)S(1)}, s32[8]{0:T(128)}, u32[]{:S(2)}) copy-start(s32[8]{0:T(128)} %copy-done.11) | copy-start | bytes 100
  303.4 125.2 %copy-start.1 = (bf16[384,1280]{1,0:T(8,128)(2,1)S(1)}, bf16[384,1280]{1,0:T(8,128)(2,1)}, u32[]{:S(2)}) copy-start(bf16[384,1280]{1,0:T(8,128)(2,1)} %param.11) | copy-start | bytes 2949124
Sparse Core Ops, SparseCore 0:
  11.1 91.8 all-gather.2
  187.7 239.0 all-reduce.2
where the time goes:
time: 437 us; the launch traced here: 435 us
  waiting for transfers between devices  183 us (42%)
  blocking collectives  101 us (23%)
  matrix products  64.1 us (15%)
  local copies, waits for them, and re-layouts  53.5 us (12%)
  between operations  14.2 us (3%)
  starting transfers between devices  9.72 us (2%)
  other arithmetic  9.7 us (2%)
    unnamed x3, waiting for transfers between devices  116 us
    psum x1, blocking collectives, on_device(): grad_gain = lax.psum(jnp.sum(d_normed * standard, axis=0), ('dp', 'inner'))  90.4 us
    all_to_all x1, waiting for transfers between devices, on_device(): lax.all_to_all(returning, 'dp', split_axis=0, concat_axis=0, tiled=True)  36.8 us
    all_gather x1, waiting for transfers between devices, on_device(): lax.all_gather(qkv_weight, ('dp', 'inner'), axis=0, tiled=True)  30.3 us
    unnamed x33, local copies, waits for them, and re-layouts  25.8 us
    dot_general x1, matrix products, on_device(): lax.dot_general(d_qkv, lax.all_gather(qkv_weight, ('dp', 'inner'), axis=0...  11 us
    all_to_all x1, blocking collectives, on_device(): lax.all_to_all(sent_flags, 'dp', split_axis=0, concat_axis=0, tiled=True)  10.3 us
    another operation x1, local copies, waits for them, and re-layouts, split_heads(): qkv_tiles.reshape(qkv_tiles.shape[0], qkv_tiles.shape[1], 3, HEADS, HDIM)  10.1 us
  transfers between devices with their start and end apart: 4, of which 3 were waited for; matrix products, arithmetic and copies ran while one was open for 9% of the time, Pallas kernels for 0%

commit v1 on v0

v1 whole, which is shorter than its diff:
```python
import functools

import jax
import jax.numpy as jnp
from jax import lax
from jax.experimental import pallas as pl
from jax.experimental.pallas import tpu as pltpu
from jax.sharding import PartitionSpec as P

D = 1280
HEADS = 16
HDIM = 80
TILE = 128
TILES = 3
N_DP = 8
N_INNER = 16
ROWS = TILES * TILE
PAIR_ROWS = 2 * ROWS
HALF = D // 2
COLS = 3 * HALF
OWN = 10
BLOCK = 80
PART = 160
PIECES = 8
STRIP = 16
MSG = 16
EPS = 1e-6
MASKED = -1e30
SCALE = HDIM ** (-0.5)
LOG2E = 1.4426950408889634
BF = jnp.bfloat16
F32 = jnp.float32
VM = pl.BlockSpec(memory_space=pltpu.VMEM)
SM = pl.BlockSpec(memory_space=pltpu.SMEM)
ANY = pl.BlockSpec(memory_space=pl.ANY)
NT = (((1,), (1,)), ((), ()))
TN = (((0,), (0,)), ((), ()))
NN = (((1,), (0,)), ((), ()))


def params(mib, **more):
    return pltpu.CompilerParams(vmem_limit_bytes=mib * 2**20, **more)


def cost(flops, nbytes, trans=0):
    return pl.CostEstimate(
        flops=flops // 1000, bytes_accessed=nbytes // 1000, transcendentals=trans // 1000
    )


def dot(a, b, dims=NN):
    return lax.dot_general(a, b, dims, preferred_element_type=F32)


def norm_rows(rows):
    wide = rows.astype(F32)
    centred = wide - jnp.mean(wide, axis=-1, keepdims=True)
    variance = jnp.mean(centred * centred, axis=-1, keepdims=True)
    inv_std = lax.rsqrt(variance + EPS)
    return centred * inv_std, inv_std


def build_order(nat_ref, perm_ref):
    for a in range(5):
        cols = slice(256 * a, 256 * (a + 1))
        feature = lax.broadcasted_iota(jnp.int32, (D, 256), 1) + 256 * a
        perm_ref[:, cols] = jnp.where(nat_ref[...] == feature, 1.0, 0.0).astype(BF)


def prep_kernel(patches_ref, gain_ref, nat_ref, normed_ref, normed_t_ref, perm_ref):
    build_order(nat_ref, perm_ref)
    standard, _ = norm_rows(patches_ref[...])
    normed = (standard * gain_ref[...]).astype(BF)
    normed_ref[...] = dot(normed, perm_ref[...], NT).astype(BF)
    normed_t_ref[...] = dot(perm_ref[...], normed, NT).astype(BF)


def prep(patches, gain, nat):
    return pl.pallas_call(
        prep_kernel,
        in_specs=[VM] * 3,
        out_specs=[VM] * 2,
        out_shape=[
            jax.ShapeDtypeStruct((ROWS, D), BF),
            jax.ShapeDtypeStruct((D, ROWS), BF),
        ],
        scratch_shapes=[pltpu.VMEM((D, D), BF)],
        compiler_params=params(32),
        cost_estimate=cost(4 * ROWS * D * D, 6 * ROWS * D),
        name="prep",
    )(patches, gain, nat)


def build_kernel(own_ref, w_ref, seg_ref, out_ref):
    lane = lax.broadcasted_iota(jnp.int32, (1, TILE), 1)
    owners = jnp.zeros((1, TILE), jnp.int32)
    for t in range(TILES):
        owners = jnp.where(lane == t, own_ref[t], owners)
    for d in range(N_DP):
        out_ref[d, OWN:MSG, :] = jnp.zeros((MSG - OWN, COLS), BF)
        for t in range(TILES):
            out_ref[d, OWN : OWN + 1, TILE * t : TILE * (t + 1)] = (
                seg_ref[t : t + 1, :].astype(F32).astype(BF)
            )
        out_ref[d, OWN + 1 : OWN + 2, 0:TILE] = owners.astype(F32).astype(BF)
        for a in range(3):
            start = D * a + HALF * (d % 2)
            out_ref[d, 0:OWN, HALF * a : HALF * (a + 1)] = w_ref[:, start : start + HALF]


def build(owners, weight, segments):
    return pl.pallas_call(
        build_kernel,
        in_specs=[SM, VM, VM],
        out_specs=VM,
        out_shape=jax.ShapeDtypeStruct((N_DP, MSG, COLS), BF),
        cost_estimate=cost(0, 2 * N_DP * MSG * COLS),
        name="build",
    )(owners, weight, segments)


def compact_kernel(group_ref, msg_ref, w_ref, seg_ref, own_ref):
    group = group_ref[0]
    seg_ref[...] = jnp.zeros_like(seg_ref)
    for s in range(N_DP):
        w_ref[OWN * s : OWN * (s + 1), :] = msg_ref[s, 0:OWN, :]
        own_ref[s : s + 1, :] = msg_ref[s, OWN + 1 : OWN + 2, 0:TILE].astype(F32)
    for rel in range(2):
        src = group + rel * (1 - 2 * (group % 2))
        for t in range(TILES):
            seg_ref[TILES * rel + t : TILES * rel + t + 1, :] = msg_ref[
                src, OWN : OWN + 1, TILE * t : TILE * (t + 1)
            ].astype(F32)


def compact(group, messages):
    return pl.pallas_call(
        compact_kernel,
        in_specs=[SM, VM],
        out_specs=[VM] * 3,
        out_shape=[
            jax.ShapeDtypeStruct((BLOCK, COLS), BF),
            jax.ShapeDtypeStruct((8, TILE), F32),
            jax.ShapeDtypeStruct((N_DP, TILE), F32),
        ],
        cost_estimate=cost(0, 4 * N_DP * MSG * COLS),
        name="compact",
    )(group, messages)


def pack_kernel(first_ref, second_ref, out_ref):
    out_ref[:BLOCK, :] = first_ref[...]
    out_ref[BLOCK:, :] = second_ref[...]


def pack(first, second):
    return pl.pallas_call(
        pack_kernel,
        in_specs=[VM] * 2,
        out_specs=VM,
        out_shape=jax.ShapeDtypeStruct((PART, COLS), BF),
        cost_estimate=cost(0, 4 * PART * COLS),
        name="pack",
    )(first, second)


def to_heads_kernel(fwd_ref, in_ref, out_ref):
    for d in range(N_DP):
        half = slice(HALF * (d % 2), HALF * (d % 2 + 1))
        for k in range(2 * TILES):
            u = TILES * (2 * (d // 2) + ((d % 2) ^ (k // TILES))) + k % TILES
            out_ref[d, k] = in_ref[fwd_ref[u], :, half]


def to_heads(fwd, strips):
    return pl.pallas_call(
        to_heads_kernel,
        in_specs=[SM, VM],
        out_specs=VM,
        out_shape=jax.ShapeDtypeStruct((N_DP, 2 * TILES, STRIP, HALF), BF),
        cost_estimate=cost(0, 4 * ROWS * D),
        name="to_heads",
    )(fwd, strips)


def to_owners_kernel(left_ref, right_ref, in_ref, out_ref):
    for v in range(N_DP * TILES):
        out_ref[v, :, :HALF] = in_ref[left_ref[v]]
        out_ref[v, :, HALF:] = in_ref[right_ref[v]]


def to_owners(left, right, strips):
    return pl.pallas_call(
        to_owners_kernel,
        in_specs=[SM, SM, VM],
        out_specs=VM,
        out_shape=jax.ShapeDtypeStruct((N_DP * TILES, STRIP, D), BF),
        cost_estimate=cost(0, 4 * ROWS * D),
        name="to_owners",
    )(left, right, strips)


def window_masks(i):
    lane = lax.broadcasted_iota(jnp.int32, (TILE, 256), 1)
    start = 32 * i
    first = (lane >= start) & (lane < start + HDIM)
    second = (lane >= start + HDIM) & (lane < start + 2 * HDIM)
    return first, second


def stack_heads(window, masks):
    zero = jnp.zeros_like(window)
    return jnp.concatenate([jnp.where(m, window, zero) for m in masks], axis=0)


def pick_heads(stacked, masks):
    zero = jnp.zeros((TILE, 256), F32)
    return jnp.where(
        masks[0], stacked[:TILE], jnp.where(masks[1], stacked[TILE:], zero)
    )


def halves(fn, *arrays):
    return jnp.concatenate(
        [fn(*(a[:, :TILE] for a in arrays)), fn(*(a[:, TILE:] for a in arrays))], axis=1
    )


def wide_max(a):
    return jnp.broadcast_to(jnp.max(a, axis=-1, keepdims=True), a.shape)


def wide_sum(a):
    return jnp.broadcast_to(jnp.sum(a, axis=-1, keepdims=True), a.shape)


def load_weight(pieces, weight, sems):
    start, copies = 0, []
    for b, piece in enumerate(pieces):
        n = piece.shape[0]
        copies.append(
            pltpu.make_async_copy(piece, weight.at[pl.ds(start, n)], sems.at[b])
        )
        start += n
    return copies


def columns(body):
    @pl.loop(0, 2)
    def _(n):
        body(pl.ds(pl.multiple_of(n * 768, 256), 768))

    body(pl.ds(1536, 384))


def main_kernel(
    normed_ref,
    partner_ref,
    seg_ref,
    normed_t_ref,
    partner_t_ref,
    cot_ref,
    *refs,
):
    pieces, (slots_ref, dqkv_ref), grads = refs[:8], refs[8:10], refs[10:12]
    qkv, cot, weight, normed_t, sems, w_sems, t_sem = refs[12:]
    t_copies = load_features(4, 2, (normed_t_ref, partner_t_ref), normed_t, t_sem)
    cot_copies = [
        pltpu.make_async_copy(cot_ref.at[j], cot.at[:, j], sems.at[j])
        for j in range(N_DP)
    ]
    w_copies = load_weight(pieces, weight, w_sems)
    for copy in w_copies + cot_copies + t_copies:
        copy.start()
    for copy in w_copies:
        copy.wait()

    def project(cols):
        qkv[:ROWS, cols] = dot(normed_ref[...], weight[:, cols]).astype(BF)
        qkv[ROWS:, cols] = dot(partner_ref[...], weight[:, cols]).astype(BF)

    columns(project)
    for copy in cot_copies:
        copy.wait()

    @pl.loop(0, 2 * TILES)
    def _(t):
        rows = pl.ds(pl.multiple_of(t * TILE, TILE), TILE)
        seg = jnp.broadcast_to(seg_ref[pl.ds(t, 1), :], (TILE, TILE))
        same = seg == seg.T
        same = jnp.concatenate([same, same], axis=1)
        pairs = range(4)
        masks = [window_masks(i) for i in pairs]
        windows = [slice(128 * i, 128 * i + 256) for i in pairs]

        def window(a, i):
            return qkv[rows, HALF * a + 128 * i : HALF * a + 128 * i + 256]

        q = [window(0, i) for i in pairs]
        d_out = [cot[t, :, :, windows[i]].reshape(TILE, 256) for i in pairs]
        kk = [stack_heads(window(1, i), masks[i]) for i in pairs]
        vv = [stack_heads(window(2, i), masks[i]) for i in pairs]
        scores = [dot(q[i], kk[i], NT) for i in pairs]
        d_probs = [dot(d_out[i], vv[i], NT) for i in pairs]
        scores = [jnp.where(same, x * (SCALE * LOG2E), MASKED) for x in scores]
        tops = [halves(wide_max, x) for x in scores]
        expo = [jnp.exp2(x - m) for x, m in zip(scores, tops)]
        sums = [halves(wide_sum, x) for x in expo]
        weights = [x * (1.0 / total) for x, total in zip(expo, sums)]
        rounded = [x.astype(BF) for x in weights]
        outs = [dot(rounded[i], vv[i]) for i in pairs]
        dvs = [dot(rounded[i], d_out[i], TN) for i in pairs]
        inner = [halves(wide_sum, d_probs[i] * weights[i]) for i in pairs]
        d_scores = [
            (weights[i] * (d_probs[i] - inner[i]) * SCALE).astype(BF) for i in pairs
        ]
        dqs = [dot(d_scores[i], kk[i]) for i in pairs]
        dks = [dot(d_scores[i], q[i], TN) for i in pairs]
        dks = [pick_heads(dks[i], masks[i]) for i in pairs]
        dvs = [pick_heads(dvs[i], masks[i]) for i in pairs]

        def lanes(vals):
            parts = [vals[0][:, :TILE]]
            for i in range(3):
                parts.append(vals[i][:, TILE:] + vals[i + 1][:, :TILE])
            parts.append(vals[3][:, TILE:])
            return jnp.concatenate([p.astype(BF) for p in parts], axis=1)

        out = lanes(outs)
        for j in range(N_DP):
            slots_ref[j, t] = out[STRIP * j : STRIP * (j + 1)]
        for a, vals in enumerate((dqs, dks, dvs)):
            dqkv_ref[rows, HALF * a : HALF * (a + 1)] = lanes(vals)

    for copy in t_copies:
        copy.wait()
    columns(functools.partial(gradient, normed_t, dqkv_ref, grads, ()))


def load_features(first, count, refs, normed_t, sems):
    return [
        pltpu.make_async_copy(
            ref.at[pl.ds(first * PART, count * PART)],
            normed_t.at[:, pl.ds(ROWS * h, ROWS)],
            sems.at[h],
        )
        for h, ref in enumerate(refs)
    ]


def gradient(normed_t, dqkv_ref, outs, arrived, cols):
    for n, out in enumerate(outs):
        part = dot(normed_t[PART * n : PART * (n + 1), :], dqkv_ref[:, cols])
        if arrived:
            part = part + arrived[n][:, cols].astype(F32)
        out[:, cols] = part.astype(BF)


def main(normed, seg, normed_t, cot, pieces):
    return pl.pallas_call(
        main_kernel,
        in_specs=[VM] * 3 + [ANY] * 3 + [ANY] * PIECES,
        out_specs=[VM] * 4,
        out_shape=[
            jax.ShapeDtypeStruct((N_DP, 2 * TILES, STRIP, HALF), BF),
            jax.ShapeDtypeStruct((PAIR_ROWS, COLS), BF),
        ]
        + [jax.ShapeDtypeStruct((PART, COLS), BF)] * 2,
        scratch_shapes=[
            pltpu.VMEM((PAIR_ROWS, COLS), BF),
            pltpu.VMEM((2 * TILES, N_DP, STRIP, HALF), BF),
            pltpu.VMEM((D, COLS), BF),
            pltpu.VMEM((2 * PART, PAIR_ROWS), BF),
            pltpu.SemaphoreType.DMA((N_DP,)),
            pltpu.SemaphoreType.DMA((PIECES,)),
            pltpu.SemaphoreType.DMA((2,)),
        ],
        compiler_params=params(58),
        cost_estimate=cost(8 * 10**9, 20 * 2**20, 10**6),
        name="main",
    )(*normed, seg, *normed_t, cot, *pieces)


def grads_kernel(firsts, normed_t_ref, partner_t_ref, dqkv_ref, *refs):
    arrived, outs, (normed_t, sems) = refs[:-4], refs[-4:-2], refs[-2:]
    copies = []
    for n, first in enumerate(firsts):
        copies += load_features(
            first,
            1,
            (normed_t_ref, partner_t_ref),
            normed_t.at[pl.ds(PART * n, PART)],
            sems.at[n],
        )
    for copy in copies:
        copy.start()
    for copy in copies:
        copy.wait()
    columns(functools.partial(gradient, normed_t, dqkv_ref, outs, arrived))


def grads(firsts, normed_t, dqkv, arrived=()):
    return pl.pallas_call(
        functools.partial(grads_kernel, firsts),
        in_specs=[ANY, ANY, VM] + [VM] * len(arrived),
        out_specs=[VM] * 2,
        out_shape=[jax.ShapeDtypeStruct((PART, COLS), BF)] * 2,
        scratch_shapes=[
            pltpu.VMEM((2 * PART, PAIR_ROWS), BF),
            pltpu.SemaphoreType.DMA((2, 2)),
        ],
        compiler_params=params(32),
        cost_estimate=cost(4 * PART * PAIR_ROWS * COLS, 5 * 2**20),
        name="grads",
    )(*normed_t, dqkv, *arrived)


def back_kernel(dqkv_ref, nat_ref, *refs):
    pieces, (out_ref, weight, perm_ref, sems) = refs[:PIECES], refs[PIECES:]
    copies = load_weight(pieces, weight, sems)
    for copy in copies:
        copy.start()
    build_order(nat_ref, perm_ref)
    for copy in copies:
        copy.wait()
    for half in (1, 0):
        rows = slice(ROWS * half, ROWS * (half + 1))
        d_normed = dot(dqkv_ref[rows, :], weight[...], NT).astype(BF)
        out_ref[half] = dot(d_normed, perm_ref[...]).astype(BF)


def back(dqkv, pieces, nat):
    return pl.pallas_call(
        back_kernel,
        in_specs=[VM, VM] + [ANY] * PIECES,
        out_specs=VM,
        out_shape=jax.ShapeDtypeStruct((2, ROWS, D), BF),
        scratch_shapes=[
            pltpu.VMEM((D, COLS), BF),
            pltpu.VMEM((D, D), BF),
            pltpu.SemaphoreType.DMA((PIECES,)),
        ],
        compiler_params=params(48),
        cost_estimate=cost(2 * PAIR_ROWS * D * (D + COLS), 15 * 2**20),
        name="back",
    )(dqkv, nat, *pieces)


def rows_kernel(patches_ref, gain_ref, mine_ref, other_ref, out_ref, gain_grad_ref):
    standard, inv_std = norm_rows(patches_ref[...])
    d_normed = mine_ref[...].astype(F32) + other_ref[...].astype(F32)
    scaled = d_normed * gain_ref[...]
    back_rows = inv_std * (
        scaled
        - jnp.mean(scaled, axis=-1, keepdims=True)
        - standard * jnp.mean(scaled * standard, axis=-1, keepdims=True)
    )
    out_ref[...] = back_rows.astype(BF)
    part = jnp.sum(d_normed * standard, axis=0, keepdims=True)

    @pl.when(pl.program_id(0) == 0)
    def _():
        gain_grad_ref[...] = jnp.zeros_like(gain_grad_ref)

    for k in range(D // TILE):
        gain_grad_ref[0, k : k + 1, :] += part[:, TILE * k : TILE * (k + 1)]

    @pl.when(pl.program_id(0) == TILES - 1)
    def _():
        for m in range(1, N_INNER):
            gain_grad_ref[m] = gain_grad_ref[0]


def rows_back(patches, gain, mine, other):
    block = pl.BlockSpec((TILE, D), lambda i: (i, 0))
    one = pl.BlockSpec((1, D), lambda i: (0, 0))
    return pl.pallas_call(
        rows_kernel,
        grid=(TILES,),
        in_specs=[block, one, block, block],
        out_specs=[block, pl.BlockSpec((N_INNER, MSG, TILE), lambda i: (0, 0, 0))],
        out_shape=[
            jax.ShapeDtypeStruct((ROWS, D), BF),
            jax.ShapeDtypeStruct((N_INNER, MSG, TILE), F32),
        ],
        compiler_params=params(48),
        cost_estimate=cost(20 * ROWS * D, 8 * ROWS * D),
        name="rows_back",
    )(patches, gain, mine, other)


def split_kernel(rows_ref, one_ref, two_ref, three_ref, gain_ref, out_ref):
    gain = gain_ref[0]
    for m in range(1, N_INNER):
        gain = gain + gain_ref[m]
    hi = gain.astype(BF).astype(F32)
    lo = gain - hi
    total = rows_ref[...].astype(F32)
    for ref in (one_ref, two_ref, three_ref):
        total = total + ref[...].astype(F32)
    total = total.astype(BF)
    for s in range(N_DP):
        out_ref[s, 0:OWN, :] = total[OWN * s : OWN * (s + 1)]
        out_ref[s, OWN:MSG, :] = jnp.zeros((MSG - OWN, COLS), BF)
        for k in range(D // TILE):
            cols = slice(TILE * k, TILE * (k + 1))
            out_ref[s, OWN : OWN + 1, cols] = hi[k : k + 1].astype(BF)
            out_ref[s, OWN + 1 : OWN + 2, cols] = lo[k : k + 1].astype(BF)


def split(rows, others, gain):
    return pl.pallas_call(
        split_kernel,
        in_specs=[VM] * 5,
        out_specs=VM,
        out_shape=jax.ShapeDtypeStruct((N_DP, MSG, COLS), BF),
        cost_estimate=cost(0, 4 * N_DP * MSG * COLS),
        name="split",
    )(rows, *others, gain)


def finish_kernel(msg_ref, out_ref, gain_ref):
    both = jnp.zeros((MSG, COLS), F32)
    for half in range(2):
        total = msg_ref[half].astype(F32)
        for chip in range(1, 4):
            total = total + msg_ref[2 * chip + half].astype(F32)
        both = both + total
        for a in range(3):
            start = D * a + HALF * half
            out_ref[:, start : start + HALF] = total[0:OWN, HALF * a : HALF * (a + 1)]
    gain_ref[...] = both[OWN : OWN + 1, :D] + both[OWN + 1 : OWN + 2, :D]


def finish(messages):
    return pl.pallas_call(
        finish_kernel,
        in_specs=[VM],
        out_specs=[VM, VM],
        out_shape=[
            jax.ShapeDtypeStruct((OWN, 3 * D), F32),
            jax.ShapeDtypeStruct((1, D), F32),
        ],
        cost_estimate=cost(0, 6 * N_DP * MSG * COLS),
        name="finish",
    )(messages)


def ring_pairs(df, ds):
    pairs = []
    for d in range(N_DP):
        dx, dz = (ds, df) if d % 2 else (df, ds)
        for x in range(4):
            for z in range(4):
                src = 4 * ((x + dx) % 4) + (z + dz) % 4
                pairs.append((N_INNER * d + src, N_INNER * d + 4 * x + z))
    return pairs


def from_ring(value, df, ds):
    return lax.ppermute(value, ("dp", "inner"), ring_pairs(df, ds))


def swap_cores(value):
    return lax.ppermute(value, "dp", [(d ^ 1, d) for d in range(N_DP)])


def exchange(value, axis="dp"):
    return lax.all_to_all(value, axis, split_axis=0, concat_axis=0, tiled=True)


def add(*arrays):
    return sum(a.astype(F32) for a in arrays).astype(BF)


def on_device(patches, segments, owners, norm_gain, qkv_weight, cotangent):
    group = lax.axis_index("dp")
    inner = lax.axis_index("inner")
    core, x, z = group % 2, inner // 4, inner % 4
    gain = norm_gain.reshape(1, D)

    messages = exchange(build(owners, qkv_weight, segments))
    block, seg, owners_all = compact(group.reshape(1).astype(jnp.int32), messages)
    partner_patches = swap_cores(patches)

    ring = [block] + [from_ring(block, f, 0) for f in (1, 2, 3)]
    near_a, near_b = pack(ring[0], ring[1]), pack(ring[2], ring[3])
    above_a, below_b = from_ring(near_a, 0, 1), from_ring(near_b, 0, -1)
    above_b, below_a = from_ring(near_b, 0, 1), from_ring(near_a, 0, -1)
    far_a, far_b = from_ring(above_a, 0, 1), from_ring(below_b, 0, -1)
    pieces = [near_a, near_b, above_a, above_b, far_a, far_b, below_a, below_b]

    pos = jnp.arange(N_INNER)
    df, ds = pos % 4, pos // 4
    m = 4 * ((x + jnp.where(core == 0, df, ds)) % 4) + (
        z + jnp.where(core == 0, ds, df)
    ) % 4
    nat = (
        (jnp.arange(N_DP)[None, :, None] * N_INNER + m[:, None, None]) * OWN
        + jnp.arange(OWN)[None, None, :]
    ).reshape(D, 1)
    normed, normed_t = zip(prep(patches, gain, nat), prep(partner_patches, gain, nat))

    owner_of = owners_all[:, :TILES].astype(jnp.int32).reshape(N_DP * TILES)
    u = jnp.arange(N_DP * TILES)
    earlier = (owner_of[:, None] == owner_of[None, :]) & (
        u[None, :] // TILES < u[:, None] // TILES
    )
    fwd = (TILES * owner_of + jnp.sum(earlier, axis=1)).astype(jnp.int32)
    inv = jnp.sum(jnp.where(fwd[None, :] == u[:, None], u[None, :], 0), axis=1)
    chip, odd, t = inv // (2 * TILES), inv // TILES % 2, inv % TILES
    left = (2 * chip * 2 * TILES + odd * TILES + t).astype(jnp.int32)
    right = ((2 * chip + 1) * 2 * TILES + (1 - odd) * TILES + t).astype(jnp.int32)

    strips = exchange(
        cotangent.reshape(TILES, N_DP, STRIP, D).transpose(1, 0, 2, 3)
    )
    cot = exchange(to_heads(fwd, strips.reshape(N_DP * TILES, STRIP, D)))

    out, dqkv, far_up, far_down = main(normed, seg, normed_t, cot, pieces)

    arrived_up, arrived_down = from_ring(far_up, 0, -1), from_ring(far_down, 0, 1)
    up_b, down_a = grads((3, 6), normed_t, dqkv)
    from_up_b, from_down_a = from_ring(up_b, 0, -1), from_ring(down_a, 0, 1)
    column_a, column_b = grads((0, 1), normed_t, dqkv)
    up_a, down_b = grads((2, 7), normed_t, dqkv, (arrived_up, arrived_down))
    from_up_a, from_down_b = from_ring(up_a, 0, -1), from_ring(down_b, 0, 1)
    column_b = add(column_b, from_up_b, from_down_b)
    two, three = column_b[:BLOCK], column_b[BLOCK:]
    column_a = add(column_a, from_up_a, from_down_a)
    zero, one = column_a[:BLOCK], column_a[BLOCK:]
    others = [from_ring(two, -2, 0), from_ring(three, 1, 0), from_ring(one, -1, 0)]

    out = exchange(out)
    out = to_owners(left, right, out.reshape(N_DP * 2 * TILES, STRIP, HALF))
    out = exchange(out.reshape(N_DP, TILES, STRIP, D))
    attended = out.transpose(1, 0, 2, 3).reshape(ROWS, D)

    dqkv_later, _, _ = lax.optimization_barrier((dqkv, up_a, down_b))
    d_normed = back(dqkv_later, pieces, nat)
    from_partner = swap_cores(d_normed[1])
    grad_rows, gain_part = rows_back(patches, gain, d_normed[0], from_partner)
    gain_parts = exchange(gain_part, "inner")

    grad_qkv, grad_gain = finish(exchange(split(zero, others, gain_parts)))
    return (attended, grad_rows, grad_qkv, grad_gain.reshape(D))


def solution(mesh):
    both = ("dp", "inner")
    placed = (
        P(both, None),
        P(both, None),
        P(both),
        P(),
        P(both, None),
        P(both, None),
    )
    return jax.shard_map(
        on_device,
        mesh=mesh,
        in_specs=placed,
        out_specs=(P(both, None), P(both, None), P(both, None), P()),
        check_vma=False,
    )
```

time: 437 us -> 204 us (0.47)
  waiting for transfers between devices: 183 us -> 44.5 us
  blocking collectives: 101 us -> 0 us
  Pallas kernels: 0 us -> 68.1 us
  matrix products: 64.1 us -> 0 us
  starting transfers between devices: 9.72 us -> 62.5 us
  local copies, waits for them, and re-layouts: 53.5 us -> 20.7 us
  between operations: 14.2 us -> 0.97 us
    unnamed x3 -> x0, waiting for transfers between devices: 116 us -> none
    psum x1 -> x0, blocking collectives: 90.4 us -> none  [on_device(): grad_gain = lax.psum(jnp.sum(d_normed * standard, axis=0), ('dp', 'inner'))]
    pallas_call x0 -> x16, Pallas kernels: none -> 68.1 us  [the longest x1 18.9 us: main(): pl.pallas_call(main_kernel, in_specs=[VM] * 3 + [ANY] * 3 + [ANY] * PIECE...]
    dot_general x13 -> x0, matrix products: 64.1 us -> none  [the longest x1 11 us: on_device(): lax.dot_general(d_qkv, lax.all_gather(qkv_weight, ('dp', 'inner'), axis=0...]
    all_gather x1 -> x0, waiting for transfers between devices: 30.3 us -> none  [on_device(): lax.all_gather(qkv_weight, ('dp', 'inner'), axis=0, tiled=True)]
    all_to_all x2 -> x7, starting transfers between devices: 9.68 us -> 38.3 us  [exchange(): return lax.all_to_all(value, axis, split_axis=0, concat_axis=0, tiled=True)]
    ppermute x0 -> x20, starting transfers between devices: none -> 24.2 us  [the longest x18 21 us: from_ring(): return lax.ppermute(value, ('dp', 'inner'), ring_pairs(df, ds))]
    ppermute x0 -> x20, waiting for transfers between devices: none -> 17.8 us  [the longest x18 17.8 us: from_ring(): return lax.ppermute(value, ('dp', 'inner'), ring_pairs(df, ds))]
  transfers between devices with their start and end apart: 4 -> 27, of which waited for: 3 -> 11; matrix products, arithmetic and copies ran while one was open for 9% -> 4% of each run, Pallas kernels for 0% -> 14%
where the time goes in v1:
time: 204 us; the launch traced here: 203 us
  Pallas kernels  68.1 us (33%)
  starting transfers between devices  62.5 us (31%)
  waiting for transfers between devices  44.5 us (22%)
  local copies, waits for them, and re-layouts  20.7 us (10%)
  other arithmetic  6.33 us (3%)
    all_to_all x7, starting transfers between devices, exchange(): return lax.all_to_all(value, axis, split_axis=0, concat_axis=0, tiled=True)  38.3 us
    all_to_all x7, waiting for transfers between devices, exchange(): return lax.all_to_all(value, axis, split_axis=0, concat_axis=0, tiled=True)  26.7 us
    ppermute x18, starting transfers between devices, from_ring(): return lax.ppermute(value, ('dp', 'inner'), ring_pairs(df, ds))  21 us
    pallas_call x1, Pallas kernels, main(): pl.pallas_call(main_kernel, in_specs=[VM] * 3 + [ANY] * 3 + [ANY] * PIECE...  18.9 us
    ppermute x18, waiting for transfers between devices, from_ring(): return lax.ppermute(value, ('dp', 'inner'), ring_pairs(df, ds))  17.8 us
    unnamed x74, local copies, waits for them, and re-layouts  14.5 us
    pallas_call x1, Pallas kernels, back(): pl.pallas_call(back_kernel, in_specs=[VM, VM] + [ANY] * PIECES, out_specs...  13.4 us
    pallas_call x2, Pallas kernels, prep(): pl.pallas_call(prep_kernel, in_specs=[VM] * 3, out_specs=[VM] * 2, out_sh...  8.7 us
  transfers between devices with their start and end apart: 27, of which 11 were waited for; matrix products, arithmetic and copies ran while one was open for 4% of the time, Pallas kernels for 14%

profile of v1, /device:TPU:1, one launch (start us, length us, event | category | flops | bytes accessed | tf_op | source)
XLA Modules:
  0.0 203.1 jit_solution(3981279616127710425)
XLA Ops:
  2.5 6.0 %all-to-all-start = ((bf16[8,16,1920]{2,1,0:T(8,128)(2,1)}), bf16[8,16,1920]{2,1,0:T(8,128)(2,1)S(1)}, u32[]{:S(2)}, u32[]{:S(2)}) async-start(bf16[8,16,1920]{2,1,0:T(8,128)(2,1)} %build.1), calls=%async_computation | async-start | bytes 983040 | tf_op jit(solution)/shard_map/all_to_all | solution.py:569
  8.5 9.1 %all-to-all-done.msg_ref = bf16[8,16,1920]{2,1,0:T(8,128)(2,1)S(1)} async-done(((bf16[8,16,1920]{2,1,0:T(8,128)(2,1)}), bf16[8,16,1920]{2,1,0:T(8,128)(2,1)S(1)}, u32[]{:S(2)}, u32[]{:S(2)}) %all-to-all-start) | async-done | bytes 491552 | tf_op jit(solution)/shard_map/all_to_all | solution.py:569
  20.2 3.8 %collective-permute-start.1 = (bf16[80,1920]{1,0:T(8,128)(2,1)}, bf16[80,1920]{1,0:T(8,128)(2,1)S(1)}, u32[]{:S(2)}, u32[]{:S(2)}) collective-permute-start(bf16[80,1920]{1,0:T(8,128)(2,1)} %get-tuple-element.32.first_ref), channel_id=1, source_target_pairs={{4,0},{5,1},{6,2},{7,3},{8,4},{9,5},{10,6},{11,7},{12,8},{13,9},{1... | collective-permute-start | bytes 921608 | tf_op jit(solution)/shard_map/ppermute | solution.py:561
  26.3 4.4 %all-to-all-start.1 = ((bf16[8,3,16,1280]{3,2,1,0:T(8,128)(2,1)}), bf16[8,3,16,1280]{3,2,1,0:T(8,128)(2,1)S(1)}, u32[]{:S(2)}, u32[]{:S(2)}) async-start(bf16[8,3,16,1280]{3,2,1,0:T(8,128)(2,1)} %bitcast.16), calls=%async_computation.1 | async-start | bytes 1966080 | tf_op jit(solution)/shard_map/all_to_all | solution.py:569
  40.0 5.2 %all-to-all-done.1 = bf16[8,3,16,1280]{3,2,1,0:T(8,128)(2,1)S(1)} async-done(((bf16[8,3,16,1280]{3,2,1,0:T(8,128)(2,1)}), bf16[8,3,16,1280]{3,2,1,0:T(8,128)(2,1)S(1)}, u32[]{:S(2)}, u32[]{:S(2)}) %all-to-all-start.1) | async-done | bytes 983072 | tf_op jit(solution)/shard_map/all_to_all | solution.py:569
  48.3 5.1 %all-to-all-start.2 = ((bf16[8,6,16,640]{3,2,1,0:T(8,128)(2,1)}), bf16[8,6,16,640]{3,2,1,0:T(8,128)(2,1)}, u32[]{:S(2)}, u32[]{:S(2)}) async-start(bf16[8,6,16,640]{3,2,1,0:T(8,128)(2,1)} %to_heads.1), calls=%async_computation.2 | async-start | bytes 1966080 | tf_op jit(solution)/shard_map/all_to_all | solution.py:569
  58.0 3.8 %prep.2 = (bf16[384,1280]{1,0:T(8,128)(2,1)S(1)}, bf16[1280,384]{1,0:T(8,128)(2,1)S(1)}) custom-call(bf16[384,1280]{1,0:T(8,128)(2,1)S(1)} %copy-done.12, f32[1,1280]{1,0:T(1,128)S(1)} %reshape.203.gain_ref, s32[1280,1]{1,0:T(8,128)S(1)} %add.193.nat_ref), custom_call_target="tpu_custom_call" | custom-call | flops 2516582 | bytes 2949 | tf_op jit(solution)/shard_map/prep/pallas_call | solution.py:79
  63.7 5.0 %prep.3 = (bf16[384,1280]{1,0:T(8,128)(2,1)S(1)}, bf16[1280,384]{1,0:T(8,128)(2,1)S(1)}) custom-call(bf16[384,1280]{1,0:T(8,128)(2,1)} %collective-permute-done.patches_ref, f32[1,1280]{1,0:T(1,128)S(1)} %reshape.203.gain_ref, s32[1280,1]{1,0:T(8,128)S(1)} %add.193.nat_ref), custom_call_target="tpu_custom_call" | custom-call | flops 2516582 | bytes 2949 | tf_op jit(solution)/shard_map/prep/pallas_call | solution.py:79
  71.0 18.9 %main.1 = (bf16[8,6,16,640]{3,2,1,0:T(8,128)(2,1)}, bf16[768,1920]{1,0:T(8,128)(2,1)}, bf16[160,1920]{1,0:T(8,128)(2,1)}, bf16[160,1920]{1,0:T(8,128)(2,1)}) custom-call(bf16[384,1280]{1,0:T(8,128)(2,1)} %copy-done.17, bf16[384,1280]{1,0:T(8,128)(2,1)} %copy-done.18, f32[8,128]{1,0:T(8,128)} %get-tuple-element.29.seg_ref, bf16[1280,384]{1,0:T(8,128)(2,1)} %copy-done.2, ...), custom_call_target="tpu_custom_call" | custom-call | flops 8000000 | bytes 20971 | tf_op jit(solution)/shard_map/main/pallas_call | solution.py:360
  92.6 8.0 %collective-permute-done.10.refs_0_ = bf16[160,1920]{1,0:T(8,128)(2,1)S(1)} collective-permute-done((bf16[160,1920]{1,0:T(8,128)(2,1)}, bf16[160,1920]{1,0:T(8,128)(2,1)S(1)}, u32[]{:S(2)}, u32[]{:S(2)}) %collective-permute-start.10) | collective-permute-done | bytes 614432 | tf_op jit(solution)/shard_map/ppermute | solution.py:561
  102.5 2.6 %grads.3 = (bf16[160,1920]{1,0:T(8,128)(2,1)}, bf16[160,1920]{1,0:T(8,128)(2,1)}) custom-call(bf16[1280,384]{1,0:T(8,128)(2,1)S(1)} %copy-done.3, bf16[1280,384]{1,0:T(8,128)(2,1)S(1)} %copy-done.6, bf16[768,1920]{1,0:T(8,128)(2,1)S(1)} %copy-done, bf16[160,1920]{1,0:T(8,128)(2,1)S(1)} %collective-permute-done.10.refs_0_, ...), custom_call_target="tpu_custom_call" | custom-call | flops 943718 | bytes 5242 | tf_op jit(solution)/shard_map/grads/pallas_call | solution.py:403
  105.1 13.4 %back.1 = bf16[2,384,1280]{2,1,0:T(8,128)(2,1)} custom-call(bf16[768,1920]{1,0:T(8,128)(2,1)} %get-tuple-element.39.dqkv_ref, s32[1280,1]{1,0:T(8,128)S(1)} %add.193.nat_ref, bf16[160,1920]{1,0:T(8,128)(2,1)S(1)} %copy-done.9, bf16[160,1920]{1,0:T(8,128)(2,1)S(1)} %copy-done.11, bf16[160,1920]{1,0:T(8,128)(2,1)S(1)} %copy-done.16, ...), custom_call_target="tpu_custom_call" | custom-call | flops 6291456 | bytes 15728 | tf_op jit(solution)/shard_map/back/pallas_call | solution.py:433
  118.5 3.1 %slice_bitcast_fusion = (bf16[384,1280]{1,0:T(8,128)(2,1)}, bf16[384,1280]{1,0:T(8,128)(2,1)}) fusion(bf16[2,384,1280]{2,1,0:T(8,128)(2,1)} %back.1), kind=kLoop, calls=%fused_computation.2 | loop fusion | bytes 3932160 | tf_op jit(solution)/shard_map/squeeze | solution.py:641
  121.6 3.0 %collective-permute-start.12 = (bf16[384,1280]{1,0:T(8,128)(2,1)}, bf16[384,1280]{1,0:T(8,128)(2,1)}, u32[]{:S(2)}, u32[]{:S(2)}) collective-permute-start(bf16[384,1280]{1,0:T(8,128)(2,1)} %get-tuple-element.51), channel_id=1, source_target_pairs={{16,0},{0,16},{48,32},{32,48},{80,64},{64,80},{112,96},{96,112},{1... | collective-permute-start | bytes 2949128 | tf_op jit(solution)/shard_map/ppermute | solution.py:565
  124.6 4.7 %all-to-all-start.3 = ((bf16[8,6,16,640]{3,2,1,0:T(8,128)(2,1)}), bf16[8,6,16,640]{3,2,1,0:T(8,128)(2,1)}, u32[]{:S(2)}, u32[]{:S(2)}) async-start(bf16[8,6,16,640]{3,2,1,0:T(8,128)(2,1)} %get-tuple-element.33), calls=%async_computation.3 | async-start | bytes 1966080 | tf_op jit(solution)/shard_map/all_to_all | solution.py:569
  146.1 4.1 %rows_back.1 = (bf16[384,1280]{1,0:T(8,128)(2,1)}, f32[16,16,128]{2,1,0:T(8,128)}) custom-call(bf16[384,1280]{1,0:T(8,128)(2,1)S(1)} %copy-done.13, f32[1,1280]{1,0:T(1,128)S(1)} %reshape.203.gain_ref, bf16[384,1280]{1,0:T(8,128)(2,1)S(1)} %copy-done.14, bf16[384,1280]{1,0:T(8,128)(2,1)} %collective-permute-done.12.other_ref), custom_call_target="tpu_custom_call" | custom-call | flops 9830 | bytes 3932 | tf_op jit(solution)/shard_map/rows_back/pallas_call | solution.py:477
  150.1 5.5 %all-to-all-start.5 = ((f32[16,16,128]{2,1,0:T(8,128)}), f32[16,16,128]{2,1,0:T(8,128)S(1)}, u32[]{:S(2)}, u32[]{:S(2)}) async-start(f32[16,16,128]{2,1,0:T(8,128)} %get-tuple-element.45), calls=%async_computation.5 | async-start | bytes 262144 | tf_op jit(solution)/shard_map/all_to_all | solution.py:569
  155.7 3.0 %add_convert_fusion = (bf16[160,1920]{1,0:T(8,128)(2,1)}, bf16[160,1920]{1,0:T(8,128)(2,1)S(1)}) fusion(bf16[160,1920]{1,0:T(8,128)(2,1)} %collective-permute-done.16, bf16[160,1920]{1,0:T(8,128)(2,1)} %collective-permute-done.15, bf16[160,1920]{1,0:T(8,128)(2,1)S(1)} %copy-done.22, bf16[160,1920]{1,0:T(8,128)(2,1)} %collective-permute-done.14, ...), kind=kLoop, calls=%fused_computation | loop fusion | flops 3686400 | bytes 4915200 | tf_op jit(solution)/shard_map/convert_element_type | solution.py:573
  158.7 3.7 %all-to-all-done.5.gain_ref = f32[16,16,128]{2,1,0:T(8,128)S(1)} async-done(((f32[16,16,128]{2,1,0:T(8,128)}), f32[16,16,128]{2,1,0:T(8,128)S(1)}, u32[]{:S(2)}, u32[]{:S(2)}) %all-to-all-start.5) | async-done | bytes 131104 | tf_op jit(solution)/shard_map/all_to_all | solution.py:569
  162.4 6.7 %all-to-all-start.4 = ((bf16[8,3,16,1280]{3,2,1,0:T(8,128)(2,1)}), bf16[8,3,16,1280]{3,2,1,0:T(8,128)(2,1)S(1)}, u32[]{:S(2)}, u32[]{:S(2)}) async-start(bf16[8,3,16,1280]{3,2,1,0:T(8,128)(2,1)} %bitcast.5), calls=%async_computation.4 | async-start | bytes 1966080 | tf_op jit(solution)/shard_map/all_to_all | solution.py:569
  172.1 3.1 %collective-permute-done.18.two_ref = bf16[80,1920]{1,0:T(8,128)(2,1)S(1)} collective-permute-done((bf16[80,1920]{1,0:T(8,128)(2,1)S(1)}, bf16[80,1920]{1,0:T(8,128)(2,1)S(1)}, u32[]{:S(2)}, u32[]{:S(2)}) %collective-permute-start.18) | collective-permute-done | bytes 307232 | tf_op jit(solution)/shard_map/ppermute | solution.py:561
  177.7 3.3 %collective-permute-done.19.three_ref = bf16[80,1920]{1,0:T(8,128)(2,1)S(1)} collective-permute-done((bf16[80,1920]{1,0:T(8,128)(2,1)S(1)}, bf16[80,1920]{1,0:T(8,128)(2,1)S(1)}, u32[]{:S(2)}, u32[]{:S(2)}) %collective-permute-start.19) | collective-permute-done | bytes 307232 | tf_op jit(solution)/shard_map/ppermute | solution.py:561
  184.2 5.9 %all-to-all-start.6 = ((bf16[8,16,1920]{2,1,0:T(8,128)(2,1)}), bf16[8,16,1920]{2,1,0:T(8,128)(2,1)S(1)}, u32[]{:S(2)}, u32[]{:S(2)}) async-start(bf16[8,16,1920]{2,1,0:T(8,128)(2,1)} %split.1), calls=%async_computation.6 | async-start | bytes 983040 | tf_op jit(solution)/shard_map/all_to_all | solution.py:569
  191.0 8.1 %all-to-all-done.6.msg_ref = bf16[8,16,1920]{2,1,0:T(8,128)(2,1)S(1)} async-done(((bf16[8,16,1920]{2,1,0:T(8,128)(2,1)}), bf16[8,16,1920]{2,1,0:T(8,128)(2,1)S(1)}, u32[]{:S(2)}, u32[]{:S(2)}) %all-to-all-start.6) | async-done | bytes 491552 | tf_op jit(solution)/shard_map/all_to_all | solution.py:569
  (141 shorter events, 62.9 us)
Async XLA Ops:
  2.5 15.1 %all-to-all-start = ((bf16[8,16,1920]{2,1,0:T(8,128)(2,1)}), bf16[8,16,1920]{2,1,0:T(8,128)(2,1)S(1)}, u32[]{:S(2)}, u32[]{:S(2)}) async-start(bf16[8,16,1920]{2,1,0:T(8,128)(2,1)} %build.1), calls=%async_computation | async-start | bytes 983040 | tf_op jit(solution)/shard_map/all_to_all | solution.py:569
  20.2 11.2 %collective-permute-start.1 = (bf16[80,1920]{1,0:T(8,128)(2,1)}, bf16[80,1920]{1,0:T(8,128)(2,1)S(1)}, u32[]{:S(2)}, u32[]{:S(2)}) collective-permute-start(bf16[80,1920]{1,0:T(8,128)(2,1)} %get-tuple-element.32.first_ref), channel_id=1, source_target_pairs={{4,0},{5,1},{6,2},{7,3},{8,4},{9,5},{10,6},{11,7},{12,8},{13,9},{1... | collective-permute-start | bytes 921608 | tf_op jit(solution)/shard_map/ppermute | solution.py:561
  23.9 12.6 %collective-permute-start.3 = (bf16[80,1920]{1,0:T(8,128)(2,1)}, bf16[80,1920]{1,0:T(8,128)(2,1)S(1)}, u32[]{:S(2)}, u32[]{:S(2)}) collective-permute-start(bf16[80,1920]{1,0:T(8,128)(2,1)} %get-tuple-element.32.first_ref), channel_id=1, source_target_pairs={{12,0},{13,1},{14,2},{15,3},{0,4},{1,5},{2,6},{3,7},{4,8},{5,9},{6... | collective-permute-start | bytes 921608 | tf_op jit(solution)/shard_map/ppermute | solution.py:561
  23.9 12.6 %collective-permute-start.2 = (bf16[80,1920]{1,0:T(8,128)(2,1)}, bf16[80,1920]{1,0:T(8,128)(2,1)}, u32[]{:S(2)}, u32[]{:S(2)}) collective-permute-start(bf16[80,1920]{1,0:T(8,128)(2,1)} %get-tuple-element.32.first_ref), channel_id=1, source_target_pairs={{8,0},{9,1},{10,2},{11,3},{12,4},{13,5},{14,6},{15,7},{0,8},{1,9},... | collective-permute-start | bytes 921608 | tf_op jit(solution)/shard_map/ppermute | solution.py:561
  26.3 18.9 %all-to-all-start.1 = ((bf16[8,3,16,1280]{3,2,1,0:T(8,128)(2,1)}), bf16[8,3,16,1280]{3,2,1,0:T(8,128)(2,1)S(1)}, u32[]{:S(2)}, u32[]{:S(2)}) async-start(bf16[8,3,16,1280]{3,2,1,0:T(8,128)(2,1)} %bitcast.16), calls=%async_computation.1 | async-start | bytes 1966080 | tf_op jit(solution)/shard_map/all_to_all | solution.py:569
  30.7 33.0 %collective-permute-start = (bf16[384,1280]{1,0:T(8,128)(2,1)S(1)}, bf16[384,1280]{1,0:T(8,128)(2,1)}, u32[]{:S(2)}, u32[]{:S(2)}) collective-permute-start(bf16[384,1280]{1,0:T(8,128)(2,1)S(1)} %copy-done.12), channel_id=1, source_target_pairs={{16,0},{0,16},{48,32},{32,48},{80,64},{64,80},{112,96},{96,112},{1... | collective-permute-start | bytes 2949128 | tf_op jit(solution)/shard_map/ppermute | solution.py:565
  34.0 22.1 %collective-permute-start.4 = (bf16[160,1920]{1,0:T(8,128)(2,1)}, bf16[160,1920]{1,0:T(8,128)(2,1)S(1)}, u32[]{:S(2)}, u32[]{:S(2)}) collective-permute-start(bf16[160,1920]{1,0:T(8,128)(2,1)} %pack.2.refs_0_), channel_id=1, source_target_pairs={{1,0},{2,1},{3,2},{0,3},{5,4},{6,5},{7,6},{4,7},{9,8},{10,9},{11,1... | collective-permute-start | bytes 1843208 | tf_op jit(solution)/shard_map/ppermute | solution.py:561
  39.2 17.0 %collective-permute-start.7 = (bf16[160,1920]{1,0:T(8,128)(2,1)}, bf16[160,1920]{1,0:T(8,128)(2,1)}, u32[]{:S(2)}, u32[]{:S(2)}) collective-permute-start(bf16[160,1920]{1,0:T(8,128)(2,1)} %pack.3.refs_1_), channel_id=1, source_target_pairs={{3,0},{0,1},{1,2},{2,3},{7,4},{4,5},{5,6},{6,7},{11,8},{8,9},{9,10... | collective-permute-start | bytes 1843208 | tf_op jit(solution)/shard_map/ppermute | solution.py:561
  48.3 22.2 %all-to-all-start.2 = ((bf16[8,6,16,640]{3,2,1,0:T(8,128)(2,1)}), bf16[8,6,16,640]{3,2,1,0:T(8,128)(2,1)}, u32[]{:S(2)}, u32[]{:S(2)}) async-start(bf16[8,6,16,640]{3,2,1,0:T(8,128)(2,1)} %to_heads.1), calls=%async_computation.2 | async-start | bytes 1966080 | tf_op jit(solution)/shard_map/all_to_all | solution.py:569
  53.4 17.1 %collective-permute-start.9 = (bf16[160,1920]{1,0:T(8,128)(2,1)S(1)}, bf16[160,1920]{1,0:T(8,128)(2,1)}, u32[]{:S(2)}, u32[]{:S(2)}) collective-permute-start(bf16[160,1920]{1,0:T(8,128)(2,1)S(1)} %copy-done.8), channel_id=1, source_target_pairs={{3,0},{0,1},{1,2},{2,3},{7,4},{4,5},{5,6},{6,7},{11,8},{8,9},{9,10... | collective-permute-start | bytes 1843208 | tf_op jit(solution)/shard_map/ppermute | solution.py:561
  55.0 15.6 %collective-permute-start.5 = (bf16[160,1920]{1,0:T(8,128)(2,1)S(1)}, bf16[160,1920]{1,0:T(8,128)(2,1)}, u32[]{:S(2)}, u32[]{:S(2)}) collective-permute-start(bf16[160,1920]{1,0:T(8,128)(2,1)S(1)} %copy-done.10), channel_id=1, source_target_pairs={{1,0},{2,1},{3,2},{0,3},{5,4},{6,5},{7,6},{4,7},{9,8},{10,9},{11,1... | collective-permute-start | bytes 1843208 | tf_op jit(solution)/shard_map/ppermute | solution.py:561
  56.1 14.8 %collective-permute-start.6 = (bf16[160,1920]{1,0:T(8,128)(2,1)S(1)}, bf16[160,1920]{1,0:T(8,128)(2,1)}, u32[]{:S(2)}, u32[]{:S(2)}) collective-permute-start(bf16[160,1920]{1,0:T(8,128)(2,1)S(1)} %collective-permute-done.4.refs_2_), channel_id=1, source_target_pairs={{1,0},{2,1},{3,2},{0,3},{5,4},{6,5},{7,6},{4,7},{9,8},{10,9},{11,1... | collective-permute-start | bytes 1843208 | tf_op jit(solution)/shard_map/ppermute | solution.py:561
  56.2 14.7 %collective-permute-start.8 = (bf16[160,1920]{1,0:T(8,128)(2,1)}, bf16[160,1920]{1,0:T(8,128)(2,1)}, u32[]{:S(2)}, u32[]{:S(2)}) collective-permute-start(bf16[160,1920]{1,0:T(8,128)(2,1)} %collective-permute-done.7.refs_7_), channel_id=1, source_target_pairs={{3,0},{0,1},{1,2},{2,3},{7,4},{4,5},{5,6},{6,7},{11,8},{8,9},{9,10... | collective-permute-start | bytes 1843208 | tf_op jit(solution)/shard_map/ppermute | solution.py:561
  89.8 10.8 %collective-permute-start.10 = (bf16[160,1920]{1,0:T(8,128)(2,1)}, bf16[160,1920]{1,0:T(8,128)(2,1)S(1)}, u32[]{:S(2)}, u32[]{:S(2)}) collective-permute-start(bf16[160,1920]{1,0:T(8,128)(2,1)} %get-tuple-element.35), channel_id=1, source_target_pairs={{3,0},{0,1},{1,2},{2,3},{7,4},{4,5},{5,6},{6,7},{11,8},{8,9},{9,10... | collective-permute-start | bytes 1843208 | tf_op jit(solution)/shard_map/ppermute | solution.py:561
  90.0 10.6 %collective-permute-start.11 = (bf16[160,1920]{1,0:T(8,128)(2,1)}, bf16[160,1920]{1,0:T(8,128)(2,1)S(1)}, u32[]{:S(2)}, u32[]{:S(2)}) collective-permute-start(bf16[160,1920]{1,0:T(8,128)(2,1)} %get-tuple-element.36), channel_id=1, source_target_pairs={{1,0},{2,1},{3,2},{0,3},{5,4},{6,5},{7,6},{4,7},{9,8},{10,9},{11,1... | collective-permute-start | bytes 1843208 | tf_op jit(solution)/shard_map/ppermute | solution.py:561
  121.6 24.5 %collective-permute-start.12 = (bf16[384,1280]{1,0:T(8,128)(2,1)}, bf16[384,1280]{1,0:T(8,128)(2,1)}, u32[]{:S(2)}, u32[]{:S(2)}) collective-permute-start(bf16[384,1280]{1,0:T(8,128)(2,1)} %get-tuple-element.51), channel_id=1, source_target_pairs={{16,0},{0,16},{48,32},{32,48},{80,64},{64,80},{112,96},{96,112},{1... | collective-permute-start | bytes 2949128 | tf_op jit(solution)/shard_map/ppermute | solution.py:565
  124.6 19.2 %all-to-all-start.3 = ((bf16[8,6,16,640]{3,2,1,0:T(8,128)(2,1)}), bf16[8,6,16,640]{3,2,1,0:T(8,128)(2,1)}, u32[]{:S(2)}, u32[]{:S(2)}) async-start(bf16[8,6,16,640]{3,2,1,0:T(8,128)(2,1)} %get-tuple-element.33), calls=%async_computation.3 | async-start | bytes 1966080 | tf_op jit(solution)/shard_map/all_to_all | solution.py:569
  134.3 21.4 %collective-permute-start.14 = (bf16[160,1920]{1,0:T(8,128)(2,1)}, bf16[160,1920]{1,0:T(8,128)(2,1)}, u32[]{:S(2)}, u32[]{:S(2)}) collective-permute-start(bf16[160,1920]{1,0:T(8,128)(2,1)} %get-tuple-element.42), channel_id=1, source_target_pairs={{1,0},{2,1},{3,2},{0,3},{5,4},{6,5},{7,6},{4,7},{9,8},{10,9},{11,1... | collective-permute-start | bytes 1843208 | tf_op jit(solution)/shard_map/ppermute | solution.py:561
  135.2 20.5 %collective-permute-start.15 = (bf16[160,1920]{1,0:T(8,128)(2,1)}, bf16[160,1920]{1,0:T(8,128)(2,1)}, u32[]{:S(2)}, u32[]{:S(2)}) collective-permute-start(bf16[160,1920]{1,0:T(8,128)(2,1)} %get-tuple-element.44), channel_id=1, source_target_pairs={{3,0},{0,1},{1,2},{2,3},{7,4},{4,5},{5,6},{6,7},{11,8},{8,9},{9,10... | collective-permute-start | bytes 1843208 | tf_op jit(solution)/shard_map/ppermute | solution.py:561
  136.0 19.7 %collective-permute-start.13 = (bf16[160,1920]{1,0:T(8,128)(2,1)}, bf16[160,1920]{1,0:T(8,128)(2,1)}, u32[]{:S(2)}, u32[]{:S(2)}) collective-permute-start(bf16[160,1920]{1,0:T(8,128)(2,1)} %get-tuple-element.37), channel_id=1, source_target_pairs={{3,0},{0,1},{1,2},{2,3},{7,4},{4,5},{5,6},{6,7},{11,8},{8,9},{9,10... | collective-permute-start | bytes 1843208 | tf_op jit(solution)/shard_map/ppermute | solution.py:561
  137.4 18.3 %collective-permute-start.16 = (bf16[160,1920]{1,0:T(8,128)(2,1)}, bf16[160,1920]{1,0:T(8,128)(2,1)}, u32[]{:S(2)}, u32[]{:S(2)}) collective-permute-start(bf16[160,1920]{1,0:T(8,128)(2,1)} %get-tuple-element.38), channel_id=1, source_target_pairs={{1,0},{2,1},{3,2},{0,3},{5,4},{6,5},{7,6},{4,7},{9,8},{10,9},{11,1... | collective-permute-start | bytes 1843208 | tf_op jit(solution)/shard_map/ppermute | solution.py:561
  150.1 12.2 %all-to-all-start.5 = ((f32[16,16,128]{2,1,0:T(8,128)}), f32[16,16,128]{2,1,0:T(8,128)S(1)}, u32[]{:S(2)}, u32[]{:S(2)}) async-start(f32[16,16,128]{2,1,0:T(8,128)} %get-tuple-element.45), calls=%async_computation.5 | async-start | bytes 262144 | tf_op jit(solution)/shard_map/all_to_all | solution.py:569
  162.4 21.8 %all-to-all-start.4 = ((bf16[8,3,16,1280]{3,2,1,0:T(8,128)(2,1)}), bf16[8,3,16,1280]{3,2,1,0:T(8,128)(2,1)S(1)}, u32[]{:S(2)}, u32[]{:S(2)}) async-start(bf16[8,3,16,1280]{3,2,1,0:T(8,128)(2,1)} %bitcast.5), calls=%async_computation.4 | async-start | bytes 1966080 | tf_op jit(solution)/shard_map/all_to_all | solution.py:569
  184.2 15.0 %all-to-all-start.6 = ((bf16[8,16,1920]{2,1,0:T(8,128)(2,1)}), bf16[8,16,1920]{2,1,0:T(8,128)(2,1)S(1)}, u32[]{:S(2)}, u32[]{:S(2)}) async-start(bf16[8,16,1920]{2,1,0:T(8,128)(2,1)} %split.1), calls=%async_computation.6 | async-start | bytes 983040 | tf_op jit(solution)/shard_map/all_to_all | solution.py:569
  (40 other events, 237.4 us)
